TPU v7x, 128 devices: a whole 4x4x4 slice. The times are simulated.
128 devices in a mesh: tm: 32 (over y, x, core), hid: 4 (over z).
Axes of the slice: x: 4, y: 4, z: 4, core: 2. Of those that a mesh axis runs over, the one named last changes fastest.
Arguments:
- gate_inputs: bfloat16 [8192, 3, 4096], P('tm', None, 'hid'), may hold values from -6 to 16
- recurrent: bfloat16 [3, 4096, 4096], P(None, None, 'hid'), may hold values from -0.09375 to 0.09375
- initial_state: float32 [4096], P('hid'), may hold values from -0.9 to 0.9
- guess: bfloat16 [8192, 4096], P('tm', 'hid'), may hold values from -0.8984375 to 0.8984375
Outputs:
- trajectory: bfloat16 [8192, 4096], P('tm', 'hid')
All inputs are finite; a program needn't handle non-finite values.
Results may differ from a plain program's by a relative error of at most 0.003.
Values may be sent and summed in bfloat16 or wider, within the bound.
A program may use at most 128 MiB of HBM per device.

v0:
```python
import jax
import jax.numpy as jnp
from jax import lax
from jax.sharding import PartitionSpec as P

ITERS = 2


def from_behind(x, axis, by):
    size = lax.axis_size(axis)
    pairs = [(i, i + by) for i in range(size) if 0 <= i + by < size]
    return lax.ppermute(x, axis, pairs)


def prefix(value, axis, join, neutral):
    count, mine = (lax.axis_size(axis), lax.axis_index(axis))
    pieces = jax.tree.map(lambda part: lax.all_gather(part, axis), value)
    total = jax.tree.map(
        lambda part, zero: jnp.full_like(part, 0) + jnp.asarray(zero, part.dtype), value, neutral
    )

    def turn(position, total):
        longer = join(total, jax.tree.map(lambda part: part[position], pieces))
        return jax.tree.map(lambda new, old: jnp.where(position < mine, new, old), longer, total)

    return lax.fori_loop(0, count - 1, turn, total)


def compose(earlier, later):
    earlier_gain, earlier_shift = earlier
    later_gain, later_shift = later
    return (later_gain * earlier_gain, later_gain * earlier_shift + later_shift)


def boundary_row(states):
    return from_behind(states[-1], "tm", 1)


def per_device(gate_inputs, recurrent, initial_state, guess):
    rows = gate_inputs.shape[0]
    own = recurrent.shape[2]
    hid_index = lax.axis_index("hid")
    time_index = lax.axis_index("tm")
    own_block = lax.dynamic_slice_in_dim(recurrent, hid_index * own, own, 1)
    diagonal = jnp.diagonal(own_block, axis1=1, axis2=2).astype(jnp.float32)
    inputs = gate_inputs.astype(jnp.float32)
    states = guess.astype(jnp.float32)
    entering = initial_state
    for step in range(ITERS):
        incoming = jnp.where(time_index == 0, initial_state, boundary_row(states))
        previous = jnp.concatenate([incoming[None, :], states[:-1]], axis=0)
        empty = jnp.zeros((rows, 3, own), jnp.float32)
        piece = lax.all_gather(previous.astype(jnp.bfloat16), "hid", axis=1, tiled=True)
        weight_rows = lax.slice_in_dim(recurrent, 0, piece.shape[1], axis=1)
        total = empty + jnp.einsum(
            "tk,gko->tgo", piece, weight_rows, preferred_element_type=jnp.float32
        )
        memory = total[:, 2]
        update = jax.nn.sigmoid(inputs[:, 0] + total[:, 0])
        reset = jax.nn.sigmoid(inputs[:, 1] + total[:, 1])
        candidate = jnp.tanh(inputs[:, 2] + reset * memory)
        target = (1.0 - update) * candidate + update * previous
        slope = (
            update * (1.0 - update) * diagonal[0] * (previous - candidate)
            + (1.0 - update)
            * (1.0 - candidate * candidate)
            * (reset * (1.0 - reset) * diagonal[1] * memory + reset * diagonal[2])
            + update
        )
        offset = target - slope * previous
        gains, shifts = lax.associative_scan(compose, (slope, offset), axis=0)
        identity = (jnp.ones((own,), jnp.float32), jnp.zeros((own,), jnp.float32))
        before_gain, before_shift = prefix((gains[-1], shifts[-1]), "tm", compose, identity)
        entering = before_gain * initial_state + before_shift
        states = gains * entering[None, :] + shifts
    return states.astype(jnp.bfloat16)


def solution(mesh):
    in_specs = (P("tm", None, "hid"), P(None, None, "hid"), P("hid"), P("tm", "hid"))
    out_specs = P("tm", "hid")
    return jax.shard_map(
        per_device, mesh=mesh, in_specs=in_specs, out_specs=out_specs, check_vma=False
    )
```

profile of v0, /device:TPU:1, one launch (start us, length us, event | category | flops | bytes accessed | tf_op | source)
XLA Modules:
  0.0 480.0 jit_solution(14330377499558345989)
XLA Ops:
  7.3 4.5 collective-permute-start
  14.1 6.1 %constant_dynamic-slice_fusion.4 = bf16[3,1024,1024]{2,1,0:T(8,128)(2,1)} fusion(bf16[3,4096,1024]{2,1,0:T(8,128)(2,1)} %param.9, s32[]{:T(128)S(6)} %select_n.77), kind=kLoop, calls=%fused_computation.194 | loop fusion | bytes 12582916 | tf_op jit(solution)/shard_map/dynamic_slice | solution.py:44
  20.3 11.5 %copy.12 = bf16[3,1024,1024]{2,0,1:T(4,128)(2,1)} copy(bf16[3,1024,1024]{2,1,0:T(8,128)(2,1)} %constant_dynamic-slice_fusion.4) | data formatting | bytes 12582912
  33.6 12.5 %gather_fusion = bf16[1024,3]{0,1:T(4,128)(2,1)S(1)} fusion(bf16[3,1024,1024]{2,0,1:T(4,128)(2,1)} %copy.12, s32[1024]{0:T(1024)S(1)} %bitcast.117), kind=kCustom, calls=%fused_computation | custom fusion | bytes 20480 | tf_op jit(solution)/shard_map/jit(diagonal)/gather | solution.py:45
  47.6 12.3 %fusion.2 = f32[256,3,1024]{2,0,1:T(8,128)S(1)} fusion(bf16[3,4096,1024]{2,1,0:T(8,128)(2,1)} %param.9, bf16[256,4096]{1,0:T(8,128)(2,1)} %all-gather.7.cloned.1.call-done), kind=kOutput, calls=%fused_computation.11 | convolution fusion | flops 6442450944 | bytes 30408704 | tf_op jit(solution)/shard_map/tk,gko->tgo/dot_general | solution.py:55
  59.9 2.6 fusion.10
  62.4 3.3 slice.539
  65.7 3.2 slice.540
  68.9 3.2 slice.576
  72.2 3.2 slice.577
  75.4 2.7 fusion.69
  84.9 2.0 fusion.71
  147.0 3.3 slice.538
  150.3 3.3 slice.611
  162.9 2.2 pad.205
  169.8 2.4 pad.223
  172.1 2.3 pad.207
  180.3 2.1 add_multiply_fusion.7
  183.1 2.6 pad.224
  185.7 2.6 pad.225
  188.3 2.1 add.501
  190.3 4.6 pad.227
  196.6 2.6 pad.208
  200.9 2.1 add.478
  203.0 2.9 add_multiply_fusion.3
  206.8 4.6 pad.226
  212.2 25.9 %all-gather.1 = f32[32,1,1024]{2,1,0:T(1,128)S(1)} all-gather(f32[1,1,1024]{2,1,0:T(1,128)S(1)} %add_bitcast_fusion.2), channel_id=1, replica_groups=mesh['tm'=32,'hid'=4] {'tm'}, dimensions={0}, use_global_device_ids=true | all-gather | bytes 135168 | tf_op jit(solution)/shard_map/all_gather | solution.py:17
  238.1 4.6 pad.211
  242.7 1.9 pad_maximum_fusion.2
  244.6 4.7 pad.210
  250.1 23.1 %all-gather = f32[32,1,1024]{2,1,0:T(1,128)S(1)} all-gather(f32[1,1,1024]{2,1,0:T(1,128)S(1)} %add_bitcast_fusion.3), channel_id=1, replica_groups=mesh['tm'=32,'hid'=4] {'tm'}, dimensions={0}, use_global_device_ids=true | all-gather | bytes 135168 | tf_op jit(solution)/shard_map/all_gather | solution.py:17
  273.2 1.8 while.32
  275.1 2.6 multiply_add_fusion
  277.8 2.3 collective-permute-start.1
  281.8 33.1 %all-gather.9.cloned.1.call-done = bf16[256,4096]{1,0:T(8,128)(2,1)} async-done(((bf16[256,1024]{1,0:T(8,128)(2,1)}), bf16[256,4096]{1,0:T(8,128)(2,1)}) %all-gather.9.cloned.1.call-update) | async-done | bytes 2097168 | tf_op jit(solution)/shard_map/all_gather | solution.py:53
  314.9 12.3 %fusion = f32[256,3,1024]{2,0,1:T(8,128)S(1)} fusion(bf16[3,4096,1024]{2,1,0:T(8,128)(2,1)} %param.9, bf16[256,4096]{1,0:T(8,128)(2,1)} %all-gather.9.cloned.1.call-done), kind=kOutput, calls=%fused_computation.9 | convolution fusion | flops 6442450944 | bytes 30408704 | tf_op jit(solution)/shard_map/tk,gko->tgo/dot_general | solution.py:55
  327.2 2.6 fusion.17
  329.8 2.2 slice.620
  332.0 2.1 slice.621
  334.0 3.2 slice.657
  407.9 2.3 add_multiply_fusion.1
  410.4 25.1 %all-gather.3 = f32[32,1,1024]{2,1,0:T(1,128)S(1)} all-gather(f32[1,1,1024]{2,1,0:T(1,128)S(1)} %add_bitcast_fusion), channel_id=1, replica_groups=mesh['tm'=32,'hid'=4] {'tm'}, dimensions={0}, use_global_device_ids=true | all-gather | bytes 135168 | tf_op jit(solution)/shard_map/all_gather | solution.py:17
  435.5 2.1 pad.243
  437.6 1.9 pad_maximum_fusion.4
  439.5 4.6 pad.242
  444.9 23.9 %all-gather.2 = f32[32,1,1024]{2,1,0:T(1,128)S(1)} all-gather(f32[1,1,1024]{2,1,0:T(1,128)S(1)} %add_bitcast_fusion.1), channel_id=1, replica_groups=mesh['tm'=32,'hid'=4] {'tm'}, dimensions={0}, use_global_device_ids=true | all-gather | bytes 135168 | tf_op jit(solution)/shard_map/all_gather | solution.py:17
  468.8 1.8 while.33
  470.7 2.5 add_convert_fusion
  (468 shorter events, 173.2 us)
Async XLA Ops:
  6.5 41.0 %all-gather.7.cloned.1.call-start = ((), (), s32[]{:S(2)}) async-start(), calls=%async_computation | async-start | bytes 2621440 | tf_op jit(solution)/shard_map/all_gather | solution.py:53
  7.3 5.7 %collective-permute-start = (f32[1024]{0:T(1024)S(1)}, f32[1024]{0:T(1024)S(1)}, u32[]{:S(2)}, u32[]{:S(2)}) collective-permute-start(f32[1024]{0:T(1024)S(1)} %bitcast.138), channel_id=1, source_target_pairs={{0,4},{4,8},{8,12},{12,16},{16,20},{20,24},{24,28},{28,32},{32,36}... | collective-permute-start | bytes 12296 | tf_op jit(solution)/shard_map/ppermute | solution.py:12
  12.9 7.3 %copy-start.2 = (f32[255,1024]{1,0:T(8,128)}, f32[255,1024]{1,0:T(8,128)S(1)}, u32[]{:S(2)}) copy-start(f32[255,1024]{1,0:T(8,128)S(1)} %slice.698) | copy-start | bytes 3133444
  14.1 300.8 %all-gather.9.cloned.1.call-start = ((), (), s32[]{:S(2)}) async-start(), calls=%async_computation.1 | async-start | bytes 2621440 | tf_op jit(solution)/shard_map/all_gather | solution.py:53
  46.2 13.6 %copy-start.20 = (f32[1,1024]{1,0:T(1,128)}, f32[1,1024]{1,0:T(1,128)S(1)}, u32[]{:S(2)}) copy-start(f32[1,1024]{1,0:T(1,128)S(1)} %get-tuple-element.364) | copy-start | bytes 12292
  46.2 13.6 %copy-start.22 = (f32[1,1024]{1,0:T(1,128)}, f32[1,1024]{1,0:T(1,128)S(1)}, u32[]{:S(2)}) copy-start(f32[1,1024]{1,0:T(1,128)S(1)} %get-tuple-element.365) | copy-start | bytes 12292
  47.6 12.3 %copy-start.3 = (f32[255,1024]{1,0:T(8,128)S(1)}, f32[255,1024]{1,0:T(8,128)}, u32[]{:S(2)}) copy-start(f32[255,1024]{1,0:T(8,128)} %copy-done.2) | copy-start | bytes 3133444
  136.5 19.7 %copy-start.13 = (f32[7,1024]{1,0:T(8,128)S(1)}, f32[7,1024]{1,0:T(8,128)}, u32[]{:S(2)}) copy-start(f32[7,1024]{1,0:T(8,128)} %slice.554) | copy-start | bytes 86020
  136.5 19.7 %copy-start.14 = (f32[7,1024]{1,0:T(8,128)S(1)}, f32[7,1024]{1,0:T(8,128)}, u32[]{:S(2)}) copy-start(f32[7,1024]{1,0:T(8,128)} %slice.603) | copy-start | bytes 86020
  136.5 21.8 %copy-start.10 = (f32[15,1024]{1,0:T(8,128)S(1)}, f32[15,1024]{1,0:T(8,128)}, u32[]{:S(2)}) copy-start(f32[15,1024]{1,0:T(8,128)} %slice.550) | copy-start | bytes 184324
  140.8 14.9 %copy-start.27 = (f32[2,1024]{1,0:T(2,128)S(1)}, f32[2,1024]{1,0:T(2,128)}, u32[]{:S(2)}) copy-start(f32[2,1024]{1,0:T(2,128)} %get-tuple-element.379) | copy-start | bytes 24580
  140.8 14.9 %copy-start.26 = (f32[2,1024]{1,0:T(2,128)S(1)}, f32[2,1024]{1,0:T(2,128)}, u32[]{:S(2)}) copy-start(f32[2,1024]{1,0:T(2,128)} %get-tuple-element.378) | copy-start | bytes 24580
  140.8 15.0 %copy-start.45 = (f32[1,1024]{1,0:T(1,128)S(1)}, f32[1,1024]{1,0:T(1,128)}, u32[]{:S(2)}) copy-start(f32[1,1024]{1,0:T(1,128)} %get-tuple-element.357) | copy-start | bytes 12292
  140.8 15.0 %copy-start.46 = (f32[1,1024]{1,0:T(1,128)S(1)}, f32[1,1024]{1,0:T(1,128)}, u32[]{:S(2)}) copy-start(f32[1,1024]{1,0:T(1,128)} %get-tuple-element.358) | copy-start | bytes 12292
  140.8 15.0 %copy-start.47 = (f32[1,1024]{1,0:T(1,128)S(1)}, f32[1,1024]{1,0:T(1,128)}, u32[]{:S(2)}) copy-start(f32[1,1024]{1,0:T(1,128)} %get-tuple-element.359) | copy-start | bytes 12292
  140.8 15.0 %copy-start.48 = (f32[1,1024]{1,0:T(1,128)S(1)}, f32[1,1024]{1,0:T(1,128)}, u32[]{:S(2)}) copy-start(f32[1,1024]{1,0:T(1,128)} %get-tuple-element.360) | copy-start | bytes 12292
  140.8 15.1 %copy-start.18 = (f32[3,1024]{1,0:T(4,128)S(1)}, f32[3,1024]{1,0:T(4,128)}, u32[]{:S(2)}) copy-start(f32[3,1024]{1,0:T(4,128)} %slice.558) | copy-start | bytes 36868
  140.8 15.1 %copy-start.19 = (f32[3,1024]{1,0:T(4,128)S(1)}, f32[3,1024]{1,0:T(4,128)}, u32[]{:S(2)}) copy-start(f32[3,1024]{1,0:T(4,128)} %slice.601) | copy-start | bytes 36868
  140.8 15.1 %copy-start.40 = (f32[1,1024]{1,0:T(1,128)S(1)}, f32[1,1024]{1,0:T(1,128)}, u32[]{:S(2)}) copy-start(f32[1,1024]{1,0:T(1,128)} %slice.738) | copy-start | bytes 12292
  140.9 15.2 %copy-start.39 = (f32[1,1024]{1,0:T(1,128)S(1)}, f32[1,1024]{1,0:T(1,128)}, u32[]{:S(2)}) copy-start(f32[1,1024]{1,0:T(1,128)} %slice.712) | copy-start | bytes 12292
  176.8 5.5 %copy-start.32 = (f32[1,1024]{1,0:T(1,128)S(1)}, f32[1,1024]{1,0:T(1,128)}, u32[]{:S(2)}) copy-start(f32[1,1024]{1,0:T(1,128)} %slice.734) | copy-start | bytes 12292
  182.3 12.6 %copy-start.30 = (f32[1,1024]{1,0:T(1,128)S(1)}, f32[1,1024]{1,0:T(1,128)}, u32[]{:S(2)}) copy-start(f32[1,1024]{1,0:T(1,128)} %slice.708) | copy-start | bytes 12292
  183.1 16.2 %copy-start.6 = (f32[64,1024]{1,0:T(8,128)S(1)}, f32[64,1024]{1,0:T(8,128)}, u32[]{:S(2)}) copy-start(f32[64,1024]{1,0:T(8,128)} %add.477) | copy-start | bytes 786436
  205.9 36.8 %copy-start.28 = (f32[1,1024]{1,0:T(1,128)S(1)}, f32[1,1024]{1,0:T(1,128)}, u32[]{:S(2)}) copy-start(f32[1,1024]{1,0:T(1,128)} %slice.707) | copy-start | bytes 12292
  206.8 68.3 %copy-start.17 = (f32[1024]{0:T(1024)S(1)}, f32[1024]{0:T(1024)}, u32[]{:S(2)}) copy-start(f32[1024]{0:T(1024)} %param.10) | copy-start | bytes 12292
  277.7 3.1 copy-start
  277.8 3.1 collective-permute-start.1
  281.8 45.4 %copy-start.21 = (f32[1,1024]{1,0:T(1,128)S(1)}, f32[1,1024]{1,0:T(1,128)}, u32[]{:S(2)}) copy-start(f32[1,1024]{1,0:T(1,128)} %copy-done.20) | copy-start | bytes 12292
  281.8 45.4 %copy-start.23 = (f32[1,1024]{1,0:T(1,128)S(1)}, f32[1,1024]{1,0:T(1,128)}, u32[]{:S(2)}) copy-start(f32[1,1024]{1,0:T(1,128)} %copy-done.22) | copy-start | bytes 12292
  314.9 12.3 %copy-start.1 = (f32[256,1024]{1,0:T(8,128)S(1)}, f32[256,1024]{1,0:T(8,128)}, u32[]{:S(2)}) copy-start(f32[256,1024]{1,0:T(8,128)} %copy-done) | copy-start | bytes 3145732
  329.8 7.5 %copy-start.5 = (f32[256,1024]{1,0:T(8,128)S(1)}, f32[256,1024]{1,0:T(8,128)}, u32[]{:S(2)}) copy-start(f32[256,1024]{1,0:T(8,128)} %get-tuple-element.295) | copy-start | bytes 3145732
  341.5 56.8 %copy-start.4 = (f32[256,1024]{1,0:T(8,128)S(1)}, f32[256,1024]{1,0:T(8,128)}, u32[]{:S(2)}) copy-start(f32[256,1024]{1,0:T(8,128)} %get-tuple-element.296) | copy-start | bytes 3145732
  395.4 6.6 %copy-start.43 = (f32[1,1024]{1,0:T(1,128)S(1)}, f32[1,1024]{1,0:T(1,128)}, u32[]{:S(2)}) copy-start(f32[1,1024]{1,0:T(1,128)} %get-tuple-element.350) | copy-start | bytes 12292
  395.4 6.6 %copy-start.44 = (f32[1,1024]{1,0:T(1,128)S(1)}, f32[1,1024]{1,0:T(1,128)}, u32[]{:S(2)}) copy-start(f32[1,1024]{1,0:T(1,128)} %get-tuple-element.351) | copy-start | bytes 12292
  395.4 6.6 %copy-start.24 = (f32[2,1024]{1,0:T(2,128)S(1)}, f32[2,1024]{1,0:T(2,128)}, u32[]{:S(2)}) copy-start(f32[2,1024]{1,0:T(2,128)} %pad_add_fusion) | copy-start | bytes 24580
  395.4 6.6 %copy-start.25 = (f32[2,1024]{1,0:T(2,128)S(1)}, f32[2,1024]{1,0:T(2,128)}, u32[]{:S(2)}) copy-start(f32[2,1024]{1,0:T(2,128)} %pad_add_fusion.1) | copy-start | bytes 24580
  395.4 6.7 %copy-start.41 = (f32[1,1024]{1,0:T(1,128)S(1)}, f32[1,1024]{1,0:T(1,128)}, u32[]{:S(2)}) copy-start(f32[1,1024]{1,0:T(1,128)} %get-tuple-element.349) | copy-start | bytes 12292
  395.4 6.7 %copy-start.42 = (f32[1,1024]{1,0:T(1,128)S(1)}, f32[1,1024]{1,0:T(1,128)}, u32[]{:S(2)}) copy-start(f32[1,1024]{1,0:T(1,128)} %get-tuple-element.352) | copy-start | bytes 12292
  395.4 9.0 %copy-start.15 = (f32[7,1024]{1,0:T(8,128)S(1)}, f32[7,1024]{1,0:T(8,128)}, u32[]{:S(2)}) copy-start(f32[7,1024]{1,0:T(8,128)} %slice.635) | copy-start | bytes 86020
  395.4 9.0 %copy-start.16 = (f32[7,1024]{1,0:T(8,128)S(1)}, f32[7,1024]{1,0:T(8,128)}, u32[]{:S(2)}) copy-start(f32[7,1024]{1,0:T(8,128)} %slice.684) | copy-start | bytes 86020
  395.4 9.2 %copy-start.11 = (f32[15,1024]{1,0:T(8,128)S(1)}, f32[15,1024]{1,0:T(8,128)}, u32[]{:S(2)}) copy-start(f32[15,1024]{1,0:T(8,128)} %slice.631) | copy-start | bytes 184324
  395.4 9.2 %copy-start.12 = (f32[15,1024]{1,0:T(8,128)S(1)}, f32[15,1024]{1,0:T(8,128)}, u32[]{:S(2)}) copy-start(f32[15,1024]{1,0:T(8,128)} %slice.686) | copy-start | bytes 184324
  397.7 6.8 %copy-start.38 = (f32[1,1024]{1,0:T(1,128)S(1)}, f32[1,1024]{1,0:T(1,128)}, u32[]{:S(2)}) copy-start(f32[1,1024]{1,0:T(1,128)} %slice.794) | copy-start | bytes 12292
  397.7 6.9 %copy-start.37 = (f32[1,1024]{1,0:T(1,128)S(1)}, f32[1,1024]{1,0:T(1,128)}, u32[]{:S(2)}) copy-start(f32[1,1024]{1,0:T(1,128)} %slice.768) | copy-start | bytes 12292
  397.7 7.0 %copy-start.36 = (f32[1,1024]{1,0:T(1,128)S(1)}, f32[1,1024]{1,0:T(1,128)}, u32[]{:S(2)}) copy-start(f32[1,1024]{1,0:T(1,128)} %slice.793) | copy-start | bytes 12292
  398.3 7.4 %copy-start.9 = (f32[31,1024]{1,0:T(8,128)S(1)}, f32[31,1024]{1,0:T(8,128)}, u32[]{:S(2)}) copy-start(f32[31,1024]{1,0:T(8,128)} %slice.688) | copy-start | bytes 380932
  399.8 5.9 %copy-start.35 = (f32[1,1024]{1,0:T(1,128)S(1)}, f32[1,1024]{1,0:T(1,128)}, u32[]{:S(2)}) copy-start(f32[1,1024]{1,0:T(1,128)} %slice.792) | copy-start | bytes 12292
  407.0 3.2 copy-start.29
  (5 other events, 5.5 us)
Sparse Core Ops, SparseCore 0:
  14.2 33.3 all-gather.6
  281.9 32.9 all-gather.8
where the time goes:
time: 487 us; the launch traced here: 480 us
  local copies, waits for them, and re-layouts  218 us (45%)
  blocking collectives  98 us (20%)
  other arithmetic  79.8 us (16%)
  waiting for transfers between devices  35.2 us (7%)
  matrix products  24.5 us (5%)
  between operations  14.8 us (3%)
  starting transfers between devices  6.89 us (1%)
    slice x104, local copies, waits for them, and re-layouts, per_device(): gains, shifts = lax.associative_scan(compose, (slope, offset), axis=0)  140 us
    all_gather x4, blocking collectives, prefix(): pieces = jax.tree.map(lambda part: lax.all_gather(part, axis), value)  98 us
    pad x56, local copies, waits for them, and re-layouts, per_device(): gains, shifts = lax.associative_scan(compose, (slope, offset), axis=0)  45.2 us
    all_gather x2, waiting for transfers between devices, per_device(): lax.all_gather(previous.astype(jnp.bfloat16), 'hid', axis=1, tiled=True)  34.4 us
    mul x26, other arithmetic, compose(): return (later_gain * earlier_gain, later_gain * earlier_shift + later_shift)  32.1 us
    dot_general x2, matrix products, per_device(): jnp.einsum('tk,gko->tgo', piece, weight_rows, preferred_element_type=jnp....  24.5 us
    concatenate x27, other arithmetic, per_device(): gains, shifts = lax.associative_scan(compose, (slope, offset), axis=0)  14.6 us
    add x27, other arithmetic, per_device(): gains, shifts = lax.associative_scan(compose, (slope, offset), axis=0)  13.4 us
  transfers between devices with their start and end apart: 4, of which 3 were waited for; matrix products, arithmetic and copies ran while one was open for 7% of the time, Pallas kernels for 0%

commit v1 on v0

--- a/solution.py
+++ b/solution.py
@@ -50,7 +50,12 @@
         incoming = jnp.where(time_index == 0, initial_state, boundary_row(states))
         previous = jnp.concatenate([incoming[None, :], states[:-1]], axis=0)
         empty = jnp.zeros((rows, 3, own), jnp.float32)
-        piece = lax.all_gather(previous.astype(jnp.bfloat16), "hid", axis=1, tiled=True)
+        piece = jnp.concatenate(
+            lax.all_to_all(
+                jnp.stack([previous.astype(jnp.bfloat16)] * lax.axis_size("hid")), "hid", 0, 0
+            ),
+            axis=1,
+        )
         weight_rows = lax.slice_in_dim(recurrent, 0, piece.shape[1], axis=1)
         total = empty + jnp.einsum(
             "tk,gko->tgo", piece, weight_rows, preferred_element_type=jnp.float32

time: 487 us -> 495 us (1.016)
  local copies, waits for them, and re-layouts: 218 us -> 240 us
  between operations: 14.8 us -> 1.39 us
  starting transfers between devices: 6.89 us -> 17.2 us
  waiting for transfers between devices: 35.2 us -> 27.7 us
    all_gather x2 -> x0, waiting for transfers between devices: 34.4 us -> none  [per_device(): lax.all_gather(previous.astype(jnp.bfloat16), 'hid', axis=1, tiled=True)]
    all_to_all x0 -> x2, waiting for transfers between devices: none -> 26.9 us  [per_device(): lax.all_to_all(jnp.stack([previous.astype(jnp.bfloat16)] * lax.axis_size(...]
    reshape x0 -> x4, local copies, waits for them, and re-layouts: none -> 18 us  [per_device(): jnp.concatenate(lax.all_to_all(jnp.stack([previous.astype(jnp.bfloat16)]...]
    all_to_all x0 -> x2, starting transfers between devices: none -> 9.71 us  [per_device(): lax.all_to_all(jnp.stack([previous.astype(jnp.bfloat16)] * lax.axis_size(...]
  transfers between devices with their start and end apart: 4 -> 4, of which waited for: 3 -> 2; matrix products, arithmetic and copies ran while one was open for 7% -> 7% of each run, Pallas kernels for 0% -> 0%
where the time goes in v1:
time: 495 us; the launch traced here: 488 us
  local copies, waits for them, and re-layouts  240 us (48%)
  blocking collectives  96.6 us (20%)
  other arithmetic  78.1 us (16%)
  waiting for transfers between devices  27.7 us (6%)
  matrix products  24.7 us (5%)
  starting transfers between devices  17.2 us (3%)
    slice x104, local copies, waits for them, and re-layouts, per_device(): gains, shifts = lax.associative_scan(compose, (slope, offset), axis=0)  140 us
    all_gather x4, blocking collectives, prefix(): pieces = jax.tree.map(lambda part: lax.all_gather(part, axis), value)  96.6 us
    pad x56, local copies, waits for them, and re-layouts, per_device(): gains, shifts = lax.associative_scan(compose, (slope, offset), axis=0)  45.3 us
    mul x26, other arithmetic, compose(): return (later_gain * earlier_gain, later_gain * earlier_shift + later_shift)  32.1 us
    all_to_all x2, waiting for transfers between devices, per_device(): lax.all_to_all(jnp.stack([previous.astype(jnp.bfloat16)] * lax.axis_size(...  26.9 us
    dot_general x2, matrix products, per_device(): jnp.einsum('tk,gko->tgo', piece, weight_rows, preferred_element_type=jnp....  24.7 us
    reshape x4, local copies, waits for them, and re-layouts, per_device(): jnp.concatenate(lax.all_to_all(jnp.stack([previous.astype(jnp.bfloat16)]...  18 us
    concatenate x27, other arithmetic, per_device(): gains, shifts = lax.associative_scan(compose, (slope, offset), axis=0)  14.6 us
  transfers between devices with their start and end apart: 4, of which 2 were waited for; matrix products, arithmetic and copies ran while one was open for 7% of the time, Pallas kernels for 0%

profile of v1, /device:TPU:1, one launch (start us, length us, event | category | flops | bytes accessed | tf_op | source)
XLA Modules:
  0.0 487.5 jit_solution(17135990311919733489)
XLA Ops:
  0.7 4.5 collective-permute-start
  8.2 5.0 %all-to-all-start = ((bf16[4,256,1024]{2,1,0:T(8,128)(2,1)}), bf16[4,256,1024]{2,1,0:T(8,128)(2,1)}, u32[]{:S(2)}, u32[]{:S(2)}) async-start(bf16[4,256,1024]{2,1,0:T(8,128)(2,1)} %stack.4), calls=%async_computation | async-start | bytes 4194304 | tf_op jit(solution)/shard_map/all_to_all | solution.py:54
  13.2 6.1 %constant_dynamic-slice_fusion.4 = bf16[3,1024,1024]{2,1,0:T(8,128)(2,1)} fusion(bf16[3,4096,1024]{2,1,0:T(8,128)(2,1)} %param.9, s32[]{:T(128)S(6)} %select_n.77), kind=kLoop, calls=%fused_computation.190 | loop fusion | bytes 12582916 | tf_op jit(solution)/shard_map/dynamic_slice | solution.py:44
  19.3 11.5 %copy.14 = bf16[3,1024,1024]{2,0,1:T(4,128)(2,1)} copy(bf16[3,1024,1024]{2,1,0:T(8,128)(2,1)} %constant_dynamic-slice_fusion.4) | data formatting | bytes 12582912
  32.7 12.3 %gather_fusion = bf16[1024,3]{0,1:T(4,128)(2,1)S(1)} fusion(bf16[3,1024,1024]{2,0,1:T(4,128)(2,1)} %copy.14, s32[1024]{0:T(1024)S(1)} %bitcast.115), kind=kCustom, calls=%fused_computation | custom fusion | bytes 20480 | tf_op jit(solution)/shard_map/jit(diagonal)/gather | solution.py:45
  45.0 4.5 copy.7
  49.6 4.5 reshape.76
  54.0 12.4 %fusion.83 = f32[256,3,1024]{2,0,1:T(8,128)S(1)} fusion(bf16[256,4096,1]{1,0,2:T(8,128)(2,1)} %reshape.76, bf16[3,4096,1024]{2,1,0:T(8,128)(2,1)} %param.9), kind=kOutput, calls=%fused_computation.210 | convolution fusion | flops 6442450944 | bytes 30408704 | tf_op jit(solution)/shard_map/tk,gko->tgo/dot_general | solution.py:60
  66.5 2.6 fusion.6
  69.1 3.3 slice.539
  72.4 3.3 slice.540
  75.6 3.2 slice.576
  78.9 3.2 slice.577
  82.1 2.7 fusion.65
  153.7 3.3 slice.538
  157.0 3.3 slice.611
  169.6 2.2 pad.205
  176.4 2.4 pad.223
  178.8 2.3 pad.207
  187.0 2.1 add_multiply_fusion.7
  189.8 2.6 pad.224
  192.4 2.6 pad.225
  197.1 4.6 pad.227
  203.4 2.6 pad.208
  207.7 2.1 add.478
  209.8 2.9 add_multiply_fusion.3
  213.6 4.6 pad.226
  219.0 27.5 %all-gather.1 = f32[32,1,1024]{2,1,0:T(1,128)S(1)} all-gather(f32[1,1,1024]{2,1,0:T(1,128)S(1)} %add_bitcast_fusion.2), channel_id=1, replica_groups=mesh['tm'=32,'hid'=4] {'tm'}, dimensions={0}, use_global_device_ids=true | all-gather | bytes 135168 | tf_op jit(solution)/shard_map/all_gather | solution.py:17
  246.5 4.6 pad.211
  253.1 4.7 pad.210
  258.5 22.3 %all-gather = f32[32,1,1024]{2,1,0:T(1,128)S(1)} all-gather(f32[1,1,1024]{2,1,0:T(1,128)S(1)} %add_bitcast_fusion.3), channel_id=1, replica_groups=mesh['tm'=32,'hid'=4] {'tm'}, dimensions={0}, use_global_device_ids=true | all-gather | bytes 135168 | tf_op jit(solution)/shard_map/all_gather | solution.py:17
  282.7 2.6 multiply_add_fusion
  285.3 3.0 collective-permute-start.1
  290.8 4.7 all-to-all-start.1
  295.5 26.9 %all-to-all-done.1 = bf16[4,256,1024]{2,1,0:T(8,128)(2,1)} async-done(((bf16[4,256,1024]{2,1,0:T(8,128)(2,1)}), bf16[4,256,1024]{2,1,0:T(8,128)(2,1)}, u32[]{:S(2)}, u32[]{:S(2)}) %all-to-all-start.1) | async-done | bytes 2097184 | tf_op jit(solution)/shard_map/all_to_all | solution.py:54
  322.4 4.6 copy.9
  327.0 4.5 reshape.77
  331.5 12.3 %fusion.84 = f32[256,3,1024]{2,0,1:T(8,128)S(1)} fusion(bf16[256,4096,1]{1,0,2:T(8,128)(2,1)} %reshape.77, bf16[3,4096,1024]{2,1,0:T(8,128)(2,1)} %param.9), kind=kOutput, calls=%fused_computation.211 | convolution fusion | flops 6442450944 | bytes 30408704 | tf_op jit(solution)/shard_map/tk,gko->tgo/dot_general | solution.py:60
  343.8 2.6 fusion.13
  346.4 2.2 slice.620
  348.5 2.1 slice.621
  350.6 3.2 slice.657
  424.4 2.3 add_multiply_fusion.1
  426.9 24.7 %all-gather.3 = f32[32,1,1024]{2,1,0:T(1,128)S(1)} all-gather(f32[1,1,1024]{2,1,0:T(1,128)S(1)} %add_bitcast_fusion), channel_id=1, replica_groups=mesh['tm'=32,'hid'=4] {'tm'}, dimensions={0}, use_global_device_ids=true | all-gather | bytes 135168 | tf_op jit(solution)/shard_map/all_gather | solution.py:17
  451.7 2.1 pad.243
  455.7 4.6 pad.242
  461.1 22.1 %all-gather.2 = f32[32,1,1024]{2,1,0:T(1,128)S(1)} all-gather(f32[1,1,1024]{2,1,0:T(1,128)S(1)} %add_bitcast_fusion.1), channel_id=1, replica_groups=mesh['tm'=32,'hid'=4] {'tm'}, dimensions={0}, use_global_device_ids=true | all-gather | bytes 135168 | tf_op jit(solution)/shard_map/all_gather | solution.py:17
  485.1 2.5 add_convert_fusion
  (472 shorter events, 184.8 us)
Async XLA Ops:
  0.7 5.7 %collective-permute-start = (f32[1024]{0:T(1024)S(1)}, f32[1024]{0:T(1024)S(1)}, u32[]{:S(2)}, u32[]{:S(2)}) collective-permute-start(f32[1024]{0:T(1024)S(1)} %bitcast.136), channel_id=1, source_target_pairs={{0,4},{4,8},{8,12},{12,16},{16,20},{20,24},{24,28},{28,32},{32,36}... | collective-permute-start | bytes 12296 | tf_op jit(solution)/shard_map/ppermute | solution.py:12
  6.4 1.8 copy-start.2
  8.2 36.9 %all-to-all-start = ((bf16[4,256,1024]{2,1,0:T(8,128)(2,1)}), bf16[4,256,1024]{2,1,0:T(8,128)(2,1)}, u32[]{:S(2)}, u32[]{:S(2)}) async-start(bf16[4,256,1024]{2,1,0:T(8,128)(2,1)} %stack.4), calls=%async_computation | async-start | bytes 4194304 | tf_op jit(solution)/shard_map/all_to_all | solution.py:54
  45.0 21.5 %copy-start.20 = (f32[1,1024]{1,0:T(1,128)}, f32[1,1024]{1,0:T(1,128)S(1)}, u32[]{:S(2)}) copy-start(f32[1,1024]{1,0:T(1,128)S(1)} %get-tuple-element.364) | copy-start | bytes 12292
  45.0 21.5 %copy-start.22 = (f32[1,1024]{1,0:T(1,128)}, f32[1,1024]{1,0:T(1,128)S(1)}, u32[]{:S(2)}) copy-start(f32[1,1024]{1,0:T(1,128)S(1)} %get-tuple-element.365) | copy-start | bytes 12292
  54.0 12.5 %copy-start.3 = (f32[255,1024]{1,0:T(8,128)S(1)}, f32[255,1024]{1,0:T(8,128)}, u32[]{:S(2)}) copy-start(f32[255,1024]{1,0:T(8,128)} %copy-done.2) | copy-start | bytes 3133444
  143.2 19.6 %copy-start.13 = (f32[7,1024]{1,0:T(8,128)S(1)}, f32[7,1024]{1,0:T(8,128)}, u32[]{:S(2)}) copy-start(f32[7,1024]{1,0:T(8,128)} %slice.554) | copy-start | bytes 86020
  143.2 19.6 %copy-start.14 = (f32[7,1024]{1,0:T(8,128)S(1)}, f32[7,1024]{1,0:T(8,128)}, u32[]{:S(2)}) copy-start(f32[7,1024]{1,0:T(8,128)} %slice.603) | copy-start | bytes 86020
  143.2 21.8 %copy-start.10 = (f32[15,1024]{1,0:T(8,128)S(1)}, f32[15,1024]{1,0:T(8,128)}, u32[]{:S(2)}) copy-start(f32[15,1024]{1,0:T(8,128)} %slice.550) | copy-start | bytes 184324
  147.5 14.9 %copy-start.27 = (f32[2,1024]{1,0:T(2,128)S(1)}, f32[2,1024]{1,0:T(2,128)}, u32[]{:S(2)}) copy-start(f32[2,1024]{1,0:T(2,128)} %get-tuple-element.379) | copy-start | bytes 24580
  147.5 14.9 %copy-start.26 = (f32[2,1024]{1,0:T(2,128)S(1)}, f32[2,1024]{1,0:T(2,128)}, u32[]{:S(2)}) copy-start(f32[2,1024]{1,0:T(2,128)} %get-tuple-element.378) | copy-start | bytes 24580
  147.5 15.0 %copy-start.45 = (f32[1,1024]{1,0:T(1,128)S(1)}, f32[1,1024]{1,0:T(1,128)}, u32[]{:S(2)}) copy-start(f32[1,1024]{1,0:T(1,128)} %get-tuple-element.357) | copy-start | bytes 12292
  147.5 15.0 %copy-start.46 = (f32[1,1024]{1,0:T(1,128)S(1)}, f32[1,1024]{1,0:T(1,128)}, u32[]{:S(2)}) copy-start(f32[1,1024]{1,0:T(1,128)} %get-tuple-element.358) | copy-start | bytes 12292
  147.5 15.0 %copy-start.47 = (f32[1,1024]{1,0:T(1,128)S(1)}, f32[1,1024]{1,0:T(1,128)}, u32[]{:S(2)}) copy-start(f32[1,1024]{1,0:T(1,128)} %get-tuple-element.359) | copy-start | bytes 12292
  147.5 15.0 %copy-start.48 = (f32[1,1024]{1,0:T(1,128)S(1)}, f32[1,1024]{1,0:T(1,128)}, u32[]{:S(2)}) copy-start(f32[1,1024]{1,0:T(1,128)} %get-tuple-element.360) | copy-start | bytes 12292
  147.5 15.1 %copy-start.18 = (f32[3,1024]{1,0:T(4,128)S(1)}, f32[3,1024]{1,0:T(4,128)}, u32[]{:S(2)}) copy-start(f32[3,1024]{1,0:T(4,128)} %slice.558) | copy-start | bytes 36868
  147.5 15.1 %copy-start.19 = (f32[3,1024]{1,0:T(4,128)S(1)}, f32[3,1024]{1,0:T(4,128)}, u32[]{:S(2)}) copy-start(f32[3,1024]{1,0:T(4,128)} %slice.601) | copy-start | bytes 36868
  147.6 15.1 %copy-start.40 = (f32[1,1024]{1,0:T(1,128)S(1)}, f32[1,1024]{1,0:T(1,128)}, u32[]{:S(2)}) copy-start(f32[1,1024]{1,0:T(1,128)} %slice.738) | copy-start | bytes 12292
  147.6 15.2 %copy-start.39 = (f32[1,1024]{1,0:T(1,128)S(1)}, f32[1,1024]{1,0:T(1,128)}, u32[]{:S(2)}) copy-start(f32[1,1024]{1,0:T(1,128)} %slice.712) | copy-start | bytes 12292
  183.6 5.5 %copy-start.32 = (f32[1,1024]{1,0:T(1,128)S(1)}, f32[1,1024]{1,0:T(1,128)}, u32[]{:S(2)}) copy-start(f32[1,1024]{1,0:T(1,128)} %slice.734) | copy-start | bytes 12292
  189.1 12.6 %copy-start.30 = (f32[1,1024]{1,0:T(1,128)S(1)}, f32[1,1024]{1,0:T(1,128)}, u32[]{:S(2)}) copy-start(f32[1,1024]{1,0:T(1,128)} %slice.708) | copy-start | bytes 12292
  189.8 16.2 %copy-start.6 = (f32[64,1024]{1,0:T(8,128)S(1)}, f32[64,1024]{1,0:T(8,128)}, u32[]{:S(2)}) copy-start(f32[64,1024]{1,0:T(8,128)} %add.477) | copy-start | bytes 786436
  212.7 38.4 %copy-start.28 = (f32[1,1024]{1,0:T(1,128)S(1)}, f32[1,1024]{1,0:T(1,128)}, u32[]{:S(2)}) copy-start(f32[1,1024]{1,0:T(1,128)} %slice.707) | copy-start | bytes 12292
  213.6 69.1 %copy-start.17 = (f32[1024]{0:T(1024)S(1)}, f32[1024]{0:T(1024)}, u32[]{:S(2)}) copy-start(f32[1024]{0:T(1024)} %param.10) | copy-start | bytes 12292
  285.3 3.7 copy-start
  285.3 3.7 collective-permute-start.1
  290.8 31.6 %all-to-all-start.1 = ((bf16[4,256,1024]{2,1,0:T(8,128)(2,1)}), bf16[4,256,1024]{2,1,0:T(8,128)(2,1)}, u32[]{:S(2)}, u32[]{:S(2)}) async-start(bf16[4,256,1024]{2,1,0:T(8,128)(2,1)} %stack.5), calls=%async_computation.1 | async-start | bytes 4194304 | tf_op jit(solution)/shard_map/all_to_all | solution.py:54
  331.4 12.3 %copy-start.1 = (f32[256,1024]{1,0:T(8,128)S(1)}, f32[256,1024]{1,0:T(8,128)}, u32[]{:S(2)}) copy-start(f32[256,1024]{1,0:T(8,128)} %copy-done) | copy-start | bytes 3145732
  331.4 12.3 %copy-start.21 = (f32[1,1024]{1,0:T(1,128)S(1)}, f32[1,1024]{1,0:T(1,128)}, u32[]{:S(2)}) copy-start(f32[1,1024]{1,0:T(1,128)} %copy-done.20) | copy-start | bytes 12292
  331.4 12.3 %copy-start.23 = (f32[1,1024]{1,0:T(1,128)S(1)}, f32[1,1024]{1,0:T(1,128)}, u32[]{:S(2)}) copy-start(f32[1,1024]{1,0:T(1,128)} %copy-done.22) | copy-start | bytes 12292
  346.4 7.5 %copy-start.5 = (f32[256,1024]{1,0:T(8,128)S(1)}, f32[256,1024]{1,0:T(8,128)}, u32[]{:S(2)}) copy-start(f32[256,1024]{1,0:T(8,128)} %get-tuple-element.295) | copy-start | bytes 3145732
  358.0 56.8 %copy-start.4 = (f32[256,1024]{1,0:T(8,128)S(1)}, f32[256,1024]{1,0:T(8,128)}, u32[]{:S(2)}) copy-start(f32[256,1024]{1,0:T(8,128)} %get-tuple-element.296) | copy-start | bytes 3145732
  411.9 6.6 %copy-start.43 = (f32[1,1024]{1,0:T(1,128)S(1)}, f32[1,1024]{1,0:T(1,128)}, u32[]{:S(2)}) copy-start(f32[1,1024]{1,0:T(1,128)} %get-tuple-element.350) | copy-start | bytes 12292
  411.9 6.6 %copy-start.44 = (f32[1,1024]{1,0:T(1,128)S(1)}, f32[1,1024]{1,0:T(1,128)}, u32[]{:S(2)}) copy-start(f32[1,1024]{1,0:T(1,128)} %get-tuple-element.351) | copy-start | bytes 12292
  411.9 6.6 %copy-start.24 = (f32[2,1024]{1,0:T(2,128)S(1)}, f32[2,1024]{1,0:T(2,128)}, u32[]{:S(2)}) copy-start(f32[2,1024]{1,0:T(2,128)} %pad_add_fusion) | copy-start | bytes 24580
  411.9 6.6 %copy-start.25 = (f32[2,1024]{1,0:T(2,128)S(1)}, f32[2,1024]{1,0:T(2,128)}, u32[]{:S(2)}) copy-start(f32[2,1024]{1,0:T(2,128)} %pad_add_fusion.1) | copy-start | bytes 24580
  411.9 6.7 %copy-start.41 = (f32[1,1024]{1,0:T(1,128)S(1)}, f32[1,1024]{1,0:T(1,128)}, u32[]{:S(2)}) copy-start(f32[1,1024]{1,0:T(1,128)} %get-tuple-element.349) | copy-start | bytes 12292
  411.9 6.7 %copy-start.42 = (f32[1,1024]{1,0:T(1,128)S(1)}, f32[1,1024]{1,0:T(1,128)}, u32[]{:S(2)}) copy-start(f32[1,1024]{1,0:T(1,128)} %get-tuple-element.352) | copy-start | bytes 12292
  411.9 9.0 %copy-start.15 = (f32[7,1024]{1,0:T(8,128)S(1)}, f32[7,1024]{1,0:T(8,128)}, u32[]{:S(2)}) copy-start(f32[7,1024]{1,0:T(8,128)} %slice.635) | copy-start | bytes 86020
  412.0 9.0 %copy-start.16 = (f32[7,1024]{1,0:T(8,128)S(1)}, f32[7,1024]{1,0:T(8,128)}, u32[]{:S(2)}) copy-start(f32[7,1024]{1,0:T(8,128)} %slice.684) | copy-start | bytes 86020
  412.0 9.2 %copy-start.11 = (f32[15,1024]{1,0:T(8,128)S(1)}, f32[15,1024]{1,0:T(8,128)}, u32[]{:S(2)}) copy-start(f32[15,1024]{1,0:T(8,128)} %slice.631) | copy-start | bytes 184324
  412.0 9.2 %copy-start.12 = (f32[15,1024]{1,0:T(8,128)S(1)}, f32[15,1024]{1,0:T(8,128)}, u32[]{:S(2)}) copy-start(f32[15,1024]{1,0:T(8,128)} %slice.686) | copy-start | bytes 184324
  414.2 6.8 %copy-start.38 = (f32[1,1024]{1,0:T(1,128)S(1)}, f32[1,1024]{1,0:T(1,128)}, u32[]{:S(2)}) copy-start(f32[1,1024]{1,0:T(1,128)} %slice.794) | copy-start | bytes 12292
  414.2 6.8 %copy-start.37 = (f32[1,1024]{1,0:T(1,128)S(1)}, f32[1,1024]{1,0:T(1,128)}, u32[]{:S(2)}) copy-start(f32[1,1024]{1,0:T(1,128)} %slice.768) | copy-start | bytes 12292
  414.2 7.0 %copy-start.36 = (f32[1,1024]{1,0:T(1,128)S(1)}, f32[1,1024]{1,0:T(1,128)}, u32[]{:S(2)}) copy-start(f32[1,1024]{1,0:T(1,128)} %slice.793) | copy-start | bytes 12292
  414.8 7.3 %copy-start.9 = (f32[31,1024]{1,0:T(8,128)S(1)}, f32[31,1024]{1,0:T(8,128)}, u32[]{:S(2)}) copy-start(f32[31,1024]{1,0:T(8,128)} %slice.688) | copy-start | bytes 380932
  416.3 5.9 %copy-start.35 = (f32[1,1024]{1,0:T(1,128)S(1)}, f32[1,1024]{1,0:T(1,128)}, u32[]{:S(2)}) copy-start(f32[1,1024]{1,0:T(1,128)} %slice.792) | copy-start | bytes 12292
  423.5 3.2 copy-start.29
  (5 other events, 5.5 us)
